TPU v7x, 32 devices: a whole 2x2x4 slice. The times are simulated.
32 devices in a mesh: groups: 2 (over y), acq: 4 (over z), az: 4 (over x, core).
Axes of the slice: x: 2, y: 2, z: 4, core: 2. Of those that a mesh axis runs over, the one named last changes fastest.
Arguments:
- slc: bfloat16 [2, 8, 512, 4096], P(None, ('groups', 'acq'), 'az'), parts along dimension 1, may hold values from -8 to 8
- pairs: int32 [32, 2], P(('groups', 'acq')), parts along dimension 0, may hold values from 0 to 3, as said below
- position: int32 [8], P(('groups', 'acq')), parts along dimension 0, may hold values from 0 to 3, as said below
- ranges: int32 [32, 2], P(('groups', 'acq')), parts along dimension 0, may hold values from 0 to 512, as said below
Outputs:
- filtered: float32 [2, 32, 64, 128], P(None, ('groups', 'acq'), 'az'), parts along dimension 1
- coherence: float32 [32, 64, 128], P(('groups', 'acq'), 'az'), parts along dimension 0
There are 2 independent parts, one for each index of `groups`. A program takes and returns all parts, laid end to end along the dimension named above; each array names one. Nothing has to cross between parts.
Inputs may be any that keep to these rules, and one draw needn't show every extreme that they name: `pairs`: row p * 4 + j names as reference the acquisition stored at row p of slc; its secondaries are 4 distinct later acquisitions at most 8 later; a slot whose partner would lie past the last acquisition names the reference twice. A permutation: position[t] is the storage row of acquisition t. `ranges`: first <= last; the range is empty, (0, 0), exactly for slots that name the reference twice.
All inputs are finite; a program needn't handle non-finite values.
Results may differ from a plain program's by a relative error of at most 0.0003.
Values may be sent and summed in bfloat16 or wider, within the bound.
A program may use at most 64 MiB of HBM per device.

v0:
```python
import functools
import math

import jax
import jax.numpy as jnp
import numpy as np
from jax import lax
from jax.experimental import pallas as pl
from jax.experimental.pallas import tpu as pltpu
from jax.sharding import PartitionSpec as P

LA = 8
LR = 32
PATCH = 32
HALF = PATCH // 2
MESH = pl.DeviceIdType.MESH


def look_table(width, slots):
    looks = width // LR
    table = np.zeros((slots, width, 128), np.float32)
    for j in range(slots):
        table[j, np.arange(width), j * looks + np.arange(width) // LR] = 1.0
    return jnp.asarray(table, jnp.bfloat16)


def split_dot(values, table):
    high = values.astype(jnp.bfloat16)
    low = (values - high.astype(jnp.float32)).astype(jnp.bfloat16)
    return jnp.dot(high, table, preferred_element_type=jnp.float32) + jnp.dot(
        low, table, preferred_element_type=jnp.float32
    )


def cross_kernel(n, slots, chunks, tab, x, table, out, *scratch):
    strips = scratch[:chunks]
    power, ready, landed, own_sem, send_sem, recv_sem, back_send, back_recv = scratch[chunks:]
    me = lax.axis_index("acq")
    lines = x.shape[2]
    width = x.shape[3] // n
    looks = width // LR
    step = lines // chunks
    rows = step // LA
    barrier = pltpu.get_barrier_semaphore()

    def peer(k):
        return lax.rem(me + k, n)

    def greet(k, carry):
        pl.semaphore_signal(barrier, inc=1, device_id={"acq": peer(k)}, device_id_type=MESH)
        return carry

    def strip_copy(c, k):
        return pltpu.make_async_remote_copy(
            src_ref=x.at[:, 0, pl.ds(c * step, step), pl.ds(pl.multiple_of(peer(k) * width, 128), width)],
            dst_ref=strips[c].at[k],
            send_sem=send_sem.at[c, k],
            recv_sem=recv_sem.at[c, k],
            device_id={"acq": peer(k)},
            device_id_type=MESH,
        )

    def own_copy(c):
        return pltpu.make_async_copy(
            x.at[:, 0, pl.ds(c * step, step), pl.ds(pl.multiple_of(me * width, 128), width)],
            strips[c].at[0],
            own_sem.at[c],
        )

    def back_copy(k):
        return pltpu.make_async_remote_copy(
            src_ref=ready.at[k],
            dst_ref=landed.at[me],
            send_sem=back_send.at[k],
            recv_sem=back_recv.at[k],
            device_id={"acq": peer(k)},
            device_id_type=MESH,
        )

    for c in range(chunks):
        own_copy(c).start()
    lax.fori_loop(1, n, greet, 0)
    pl.semaphore_wait(barrier, n - 1)
    for c in range(chunks):
        def send(k, carry, c=c):
            strip_copy(c, k).start()
            return carry
        lax.fori_loop(1, n, send, 0)

    lane_slot = lax.broadcasted_iota(jnp.int32, (step, 128), 1) // looks
    first_line = lax.axis_index("az") * lines
    every_slot = table[0]
    for j in range(1, slots):
        every_slot = every_slot + table[j]

    def slot_of(row):
        return lax.rem(me - row + n, n)

    for c in range(chunks):
        own_copy(c).wait()

        def arrive(k, carry, c=c):
            strip_copy(c, k).wait_recv()
            return carry
        lax.fori_loop(1, n, arrive, 0)
        line = first_line + c * step + lax.broadcasted_iota(jnp.int32, (step, 128), 0)

        def powers(k, carry, c=c):
            re = strips[c][k, 0].astype(jnp.float32)
            im = strips[c][k, 1].astype(jnp.float32)
            power[k] = split_dot(re * re + im * im, every_slot)
            return carry
        lax.fori_loop(0, n, powers, 0)

        def pairs_of(k, carry, c=c, line=line):
            row = peer(k)
            at = slot_of(row)
            ref_re = strips[c][at, 0].astype(jnp.float32)
            ref_im = strips[c][at, 1].astype(jnp.float32)
            sum_re = jnp.zeros((step, 128), jnp.float32)
            sum_im = jnp.zeros((step, 128), jnp.float32)
            sec_power = jnp.zeros((step, 128), jnp.float32)
            alive = jnp.zeros((step, 128), jnp.float32)
            for j in range(slots):
                q = row * slots + j
                other = slot_of(tab[0, q])
                sec_re = strips[c][other, 0].astype(jnp.float32)
                sec_im = strips[c][other, 1].astype(jnp.float32)
                sum_re = sum_re + split_dot(ref_re * sec_re + ref_im * sec_im, table[j])
                sum_im = sum_im + split_dot(ref_im * sec_re - ref_re * sec_im, table[j])
                mine = lane_slot == j
                sec_power = jnp.where(mine, power[other], sec_power)
                alive = jnp.where(mine & (line >= tab[1, q]) & (line < tab[2, q]), 1.0, alive)

            def multilook(values):
                return jnp.sum((values * alive).reshape(rows, LA, 128), axis=1) / (LA * LR)

            look_re = multilook(sum_re)
            look_im = multilook(sum_im)
            denominator = jnp.maximum(jnp.sqrt(multilook(power[at]) * multilook(sec_power)), 0.5)
            coherent_re = look_re / denominator
            coherent_im = look_im / denominator
            ready[k, 0, pl.ds(c * rows, rows)] = coherent_re
            ready[k, 1, pl.ds(c * rows, rows)] = coherent_im
            ready[k, 2, pl.ds(c * rows, rows)] = jnp.sqrt(
                coherent_re * coherent_re + coherent_im * coherent_im
            )
            return carry

        def pairs_and_send(k, carry):
            pairs_of(k, carry)
            back_copy(k).start()
            return carry

        if c < chunks - 1:
            lax.fori_loop(0, n, pairs_of, 0)
        else:
            lax.fori_loop(1, n, pairs_and_send, 0)
            pairs_of(0, 0)

    def finish(k, carry):
        back_copy(k).wait_recv()
        return carry
    lax.fori_loop(1, n, finish, 0)

    lane = lax.broadcasted_iota(jnp.int32, (3, lines // LA, 128), 2) // looks
    total = [jnp.zeros((3, lines // LA, 128), jnp.float32) for _ in range(slots)]
    for d in range(n):
        piece = jnp.where(me == d, ready[0], landed[d])
        for j in range(slots):
            shift = ((d - j) * looks) % 128
            moved = pltpu.roll(piece, shift, 2) if shift else piece
            total[j] = jnp.where(lane == d, moved, total[j])
    for j in range(slots):
        out[:, j] = total[j]

    def drain(k, carry):
        for c in range(chunks):
            strip_copy(c, k).wait_send()
        back_copy(k).wait_send()
        return carry
    lax.fori_loop(1, n, drain, 0)


def coherences(slc, tab, n, slots):
    lines, samples = slc.shape[2:]
    width = samples // n
    chunks = 2
    rows = lines // LA
    return pl.pallas_call(
        functools.partial(cross_kernel, n, slots, chunks),
        out_shape=jax.ShapeDtypeStruct((3, slots, rows, 128), jnp.float32),
        in_specs=[
            pl.BlockSpec(memory_space=pltpu.SMEM),
            pl.BlockSpec(memory_space=pl.ANY),
            pl.BlockSpec(memory_space=pltpu.VMEM),
        ],
        out_specs=pl.BlockSpec(memory_space=pltpu.VMEM),
        scratch_shapes=[pltpu.VMEM((n, 2, lines // chunks, width), jnp.bfloat16)] * chunks
        + [
            pltpu.VMEM((n, lines // chunks, 128), jnp.float32),
            pltpu.VMEM((n, 3, rows, 128), jnp.float32),
            pltpu.VMEM((n, 3, rows, 128), jnp.float32),
            pltpu.SemaphoreType.DMA((chunks,)),
            pltpu.SemaphoreType.DMA((chunks, n)),
            pltpu.SemaphoreType.DMA((chunks, n)),
            pltpu.SemaphoreType.DMA((n,)),
            pltpu.SemaphoreType.DMA((n,)),
        ],
        compiler_params=pltpu.CompilerParams(
            collective_id=0, has_side_effects=True, vmem_limit_bytes=32 * 2**20
        ),
    )(tab, slc, look_table(width, slots))


def goldstein_tables(columns):
    ticks = np.arange(PATCH)
    angle = 2.0 * math.pi / PATCH * ((ticks[:, None] * ticks[None, :]) % PATCH)
    cos, sin = np.cos(angle), np.sin(angle)
    window = np.sin((ticks + 0.5) * (math.pi / PATCH)) ** 2
    left = np.block([[cos, sin], [-sin, cos]]) * np.tile(window, 2)[None, :]
    left_back = np.block([[cos, -sin], [sin, cos]]) / (PATCH * PATCH)
    eye = np.eye(columns // PATCH)
    wide_cos, wide_sin = np.kron(eye, cos), np.kron(eye, sin)
    wide_window = np.tile(window, columns // PATCH)
    forward, backward = [], []
    for offset in (0, HALF):
        keep = np.arange(columns) < (columns - PATCH if offset else columns)
        scale = (wide_window * keep)[:, None]
        into = [np.roll(scale * m, offset, axis=0) for m in (wide_cos, wide_sin)]
        forward.append(np.block([[into[0], -into[1]], [into[1], into[0]]]))
        back = [np.roll(m * keep[None, :], offset, axis=1) for m in (wide_cos, wide_sin)]
        backward.append(np.block([[back[0], back[1]], [-back[1], back[0]]]))
    ones = np.kron(eye, np.ones((PATCH, PATCH))) / (PATCH * PATCH)
    arrays = (left, left_back, np.concatenate(forward, 1), np.concatenate(backward, 0), ones)
    return tuple(jnp.asarray(a, jnp.float32) for a in arrays)


def goldstein_kernel(cells, left, left_back, forward, backward, ones, out):
    dot = functools.partial(
        jnp.dot, precision=lax.Precision.HIGHEST, preferred_element_type=jnp.float32
    )
    slots, extended, columns = cells.shape[1:]
    own = extended - 2 * HALF
    count = own // HALF + 1
    wide = dot(
        jnp.concatenate(
            [cells[0].reshape(slots * extended, columns), cells[1].reshape(slots * extended, columns)],
            axis=1,
        ),
        forward[...],
    )
    pieces = [(s, k, o) for s in range(slots) for k in range(count) for o in range(2)]

    def part(s, k, o, plane):
        row = s * extended + k * HALF
        col = (2 * o + plane) * columns
        return wide[row : row + PATCH, col : col + columns]

    stacked = jnp.concatenate(
        [jnp.concatenate([part(*p, 0) for p in pieces], axis=1),
         jnp.concatenate([part(*p, 1) for p in pieces], axis=1)],
        axis=0,
    )
    spectrum = dot(left[...], stacked)
    spec_re, spec_im = spectrum[:PATCH], spectrum[PATCH:]
    amplitude = jnp.sqrt(jnp.sqrt(spec_re * spec_re + spec_im * spec_im + 1e-06))
    sums = jnp.sum(amplitude, axis=0, keepdims=True)
    sums = jnp.concatenate(
        [sums[:, i * columns : (i + 1) * columns] for i in range(len(pieces))], axis=0
    )
    means = dot(sums, ones[...])
    means = jnp.concatenate([means[i : i + 1] for i in range(len(pieces))], axis=1)
    response = amplitude / means
    restored = dot(
        left_back[...], jnp.concatenate([response * spec_re, response * spec_im], axis=0)
    )

    def taken(s, k, o, plane, low):
        row = plane * PATCH + low
        col = pieces.index((s, k, o)) * columns
        return restored[row : row + HALF, col : col + columns]

    summed = jnp.concatenate(
        [
            jnp.concatenate(
                [
                    taken(s, r, o, plane, HALF) + taken(s, r + 1, o, plane, 0)
                    for o in range(2)
                    for plane in range(2)
                ],
                axis=1,
            )
            for s in range(slots)
            for r in range(own // HALF)
        ],
        axis=0,
    )
    result = dot(summed, backward[...])
    for plane in range(2):
        out[plane] = result[:, plane * columns : (plane + 1) * columns].reshape(slots, own, columns)


def with_halo(cells, axis, dim, width):
    count = lax.axis_size(axis)
    head = lax.slice_in_dim(cells, 0, width, axis=dim)
    tail = lax.slice_in_dim(cells, cells.shape[dim] - width, cells.shape[dim], axis=dim)
    return jnp.concatenate(
        [
            lax.ppermute(tail, axis, [(i, i + 1) for i in range(count - 1)]),
            cells,
            lax.ppermute(head, axis, [(i + 1, i) for i in range(count - 1)]),
        ],
        axis=dim,
    )


def local(slc, pairs, position, ranges):
    n = lax.axis_size("acq")
    slots = pairs.shape[0]
    mine = jnp.concatenate([pairs[:, 1], ranges[:, 0], ranges[:, 1], position])
    every = lax.all_gather(mine, "acq", axis=0, tiled=False)
    sec_time = every[:, :slots].reshape(-1)
    time_index = jnp.arange(n, dtype=jnp.int32)
    sec_row = jnp.sum(
        jnp.where(sec_time[:, None] == time_index[None, :], every[:, 3 * slots][None, :], 0), axis=1
    )
    tab = jnp.stack(
        [sec_row, every[:, slots : 2 * slots].reshape(-1), every[:, 2 * slots : 3 * slots].reshape(-1)]
    )
    planes = coherences(slc, tab, n, slots)
    extended = with_halo(planes[:2], "az", 2, HALF)
    filtered = pl.pallas_call(
        goldstein_kernel,
        out_shape=jax.ShapeDtypeStruct((2,) + planes.shape[1:], jnp.float32),
        compiler_params=pltpu.CompilerParams(vmem_limit_bytes=32 * 2**20),
    )(extended, *goldstein_tables(planes.shape[-1]))
    return (filtered, planes[2])


def solution(mesh):
    return jax.shard_map(
        local,
        mesh=mesh,
        in_specs=(
            P(None, ("groups", "acq"), "az", None),
            P(("groups", "acq"), None),
            P(("groups", "acq")),
            P(("groups", "acq"), None),
        ),
        out_specs=(P(None, ("groups", "acq"), "az", None), P(("groups", "acq"), "az", None)),
        check_vma=False,
    )
```

profile of v0, /device:TPU:1, one launch (start us, length us, event | category | flops | bytes accessed | tf_op | source)
XLA Modules:
  0.0 81.4 jit_solution(16150853309119623792)
XLA Ops:
  0.6 0.0 copy-start.4
  1.3 1.2 %dynamic-slice = u32[1]{0:T(128)} dynamic-slice(u32[32]{0:T(128)} %constant.26, u32[]{:T(128)S(6)} %add), dynamic_slice_sizes={1} | dynamic-slice | bytes 12
  3.2 0.8 slice_bitcast_fusion.2
  4.0 0.2 add_dynamic-update-slice_fusion
  4.1 7.3 %all-reduce = s32[52]{0:T(128)S(1)} all-reduce(s32[52]{0:T(128)S(1)} %add_dynamic-update-slice_fusion), channel_id=2, replica_groups=mesh['groups'=2,'acq'=4,'az'=4] {'acq'}, use_global_device_ids=true, to_apply=%add | all-reduce | flops 52 | bytes 416
  11.4 0.1 reshape.6
  11.5 0.2 slice_reduce_fusion
  11.7 0.1 fusion
  11.7 0.1 eq.15
  11.8 0.1 stack_reshape.7
  11.9 0.1 stack_reshape.6
  12.0 0.1 select_reduce_fusion
  12.1 0.0 copy-start
  12.1 1.6 %copy-done = bf16[2,1,128,4096]{3,2,1,0:T(8,128)(2,1)S(1)} copy-done((bf16[2,1,128,4096]{3,2,1,0:T(8,128)(2,1)S(1)}, bf16[2,1,128,4096]{3,2,1,0:T(8,128)(2,1)}, u32[]{:S(2)}) %copy-start) | copy-done | bytes 2097176
  13.7 0.0 copy-start.1
  13.7 1.2 %copy-done.1 = bf16[4,1024,128]{2,1,0:T(8,128)(2,1)S(1)} copy-done((bf16[4,1024,128]{2,1,0:T(8,128)(2,1)S(1)}, bf16[4,1024,128]{2,1,0:T(8,128)(2,1)}, u32[]{:S(2)}) %copy-start.1) | copy-done | bytes 1048600
  14.9 0.0 copy-start.2
  14.9 0.0 copy-start.3
  14.9 0.0 copy-start.5
  14.9 0.0 copy-start.6
  14.9 54.5 %shard_map.113 = f32[3,4,16,128]{3,2,1,0:T(8,128)S(1)} custom-call(s32[3,16]{1,0:T(4,128)S(1)} %pad_add_fusion.tab, bf16[2,1,128,4096]{3,2,1,0:T(8,128)(2,1)S(1)} %copy-done, bf16[4,1024,128]{2,1,0:T(8,128)(2,1)S(1)} %copy-done.1), custom_call_target="tpu_custom_call" | custom-call | tf_op jit(solution)/shard_map/pallas_call | solution.py:190
  69.4 4.5 %collective-permute-start.1 = (f32[2,4,16,128]{3,2,1,0:T(8,128)S(1)}, f32[2,4,16,128]{3,2,1,0:T(8,128)S(1)}, u32[]{:S(2)}, u32[]{:S(2)}) collective-permute-start(f32[2,4,16,128]{3,2,1,0:T(8,128)S(1)} %slice.34), channel_id=1, source_target_pairs={{1,0},{2,1},{3,2},{5,4},{6,5},{7,6},{9,8},{10,9},{11,10},{13,12},{... | collective-permute-start | bytes 196616 | tf_op jit(solution)/shard_map/ppermute | solution.py:312
  73.9 3.0 %collective-permute-start = (f32[2,4,16,128]{3,2,1,0:T(8,128)S(1)}, f32[2,4,16,128]{3,2,1,0:T(8,128)S(1)}, u32[]{:S(2)}, u32[]{:S(2)}) collective-permute-start(f32[2,4,16,128]{3,2,1,0:T(8,128)S(1)} %slice.34), channel_id=1, source_target_pairs={{0,1},{1,2},{2,3},{4,5},{5,6},{6,7},{8,9},{9,10},{10,11},{12,13},{... | collective-permute-start | bytes 196616 | tf_op jit(solution)/shard_map/ppermute | solution.py:310
  76.9 0.6 slice_bitcast_fusion
  77.6 0.0 collective-permute-done.1
  77.6 0.7 collective-permute-done
  78.3 0.0 copy-done.4
  78.3 0.0 copy-done.2
  78.3 0.0 copy-done.3
  78.3 0.0 copy-done.5
  78.3 0.0 copy-done.6
  78.3 3.1 %shard_map.114 = f32[2,4,16,128]{3,2,1,0:T(8,128)} custom-call(f32[2,4,48,128]{3,2,1,0:T(8,128)S(1)} %pad_maximum_fusion.cells, f32[64,64]{1,0:T(8,128)S(1)} %copy-done.6, f32[64,64]{1,0:T(8,128)S(1)} %copy-done.5, f32[256,512]{1,0:T(8,128)S(1)} %copy-done.3, f32[512,256]{1,0:T(8,128)S(1)} %copy-done.2, f32[128,128]{1,0:T(8,128)S(1)} %copy-done.4), custom_call_target="tpu_custom_call" | custom-call | tf_op jit(solution)/shard_map/pallas_call | solution.py:333
  (4 shorter events, 0.0 us)
Async XLA Ops:
  0.6 77.6 %copy-start.4 = (f32[128,128]{1,0:T(8,128)S(1)}, f32[128,128]{1,0:T(8,128)}, u32[]{:S(2)}) copy-start(f32[128,128]{1,0:T(8,128)} %constant.19.clone.ones) | copy-start | bytes 196612
  12.1 1.6 %copy-start = (bf16[2,1,128,4096]{3,2,1,0:T(8,128)(2,1)S(1)}, bf16[2,1,128,4096]{3,2,1,0:T(8,128)(2,1)}, u32[]{:S(2)}) copy-start(bf16[2,1,128,4096]{3,2,1,0:T(8,128)(2,1)} %x.2) | copy-start | bytes 6291460
  13.7 1.2 %copy-start.1 = (bf16[4,1024,128]{2,1,0:T(8,128)(2,1)S(1)}, bf16[4,1024,128]{2,1,0:T(8,128)(2,1)}, u32[]{:S(2)}) copy-start(bf16[4,1024,128]{2,1,0:T(8,128)(2,1)} %constant.14.clone.table) | copy-start | bytes 3145732
  14.9 63.4 %copy-start.2 = (f32[512,256]{1,0:T(8,128)S(1)}, f32[512,256]{1,0:T(8,128)}, u32[]{:S(2)}) copy-start(f32[512,256]{1,0:T(8,128)} %constant.18.clone.backward) | copy-start | bytes 1572868
  14.9 63.4 %copy-start.3 = (f32[256,512]{1,0:T(8,128)S(1)}, f32[256,512]{1,0:T(8,128)}, u32[]{:S(2)}) copy-start(f32[256,512]{1,0:T(8,128)} %constant.17.clone.forward) | copy-start | bytes 1572868
  14.9 63.4 %copy-start.5 = (f32[64,64]{1,0:T(8,128)S(1)}, f32[64,64]{1,0:T(8,128)}, u32[]{:S(2)}) copy-start(f32[64,64]{1,0:T(8,128)} %constant.16.clone.left_back) | copy-start | bytes 49156
  14.9 63.4 %copy-start.6 = (f32[64,64]{1,0:T(8,128)S(1)}, f32[64,64]{1,0:T(8,128)}, u32[]{:S(2)}) copy-start(f32[64,64]{1,0:T(8,128)} %constant.15.clone.left) | copy-start | bytes 49156
  69.4 8.1 %collective-permute-start.1 = (f32[2,4,16,128]{3,2,1,0:T(8,128)S(1)}, f32[2,4,16,128]{3,2,1,0:T(8,128)S(1)}, u32[]{:S(2)}, u32[]{:S(2)}) collective-permute-start(f32[2,4,16,128]{3,2,1,0:T(8,128)S(1)} %slice.34), channel_id=1, source_target_pairs={{1,0},{2,1},{3,2},{5,4},{6,5},{7,6},{9,8},{10,9},{11,10},{13,12},{... | collective-permute-start | bytes 196616 | tf_op jit(solution)/shard_map/ppermute | solution.py:312
  73.9 4.3 %collective-permute-start = (f32[2,4,16,128]{3,2,1,0:T(8,128)S(1)}, f32[2,4,16,128]{3,2,1,0:T(8,128)S(1)}, u32[]{:S(2)}, u32[]{:S(2)}) collective-permute-start(f32[2,4,16,128]{3,2,1,0:T(8,128)S(1)} %slice.34), channel_id=1, source_target_pairs={{0,1},{1,2},{2,3},{4,5},{5,6},{6,7},{8,9},{9,10},{10,11},{12,13},{... | collective-permute-start | bytes 196616 | tf_op jit(solution)/shard_map/ppermute | solution.py:310
where the time goes:
time: 81.7 us; the launch traced here: 81.4 us
  Pallas kernels  57.6 us (71%)
  starting transfers between devices  7.51 us (9%)
  blocking collectives  7.25 us (9%)
  local copies, waits for them, and re-layouts  6.05 us (7%)
  between operations  2.07 us (3%)
    pallas_call x1, Pallas kernels, coherences(): pl.pallas_call(functools.partial(cross_kernel, n, slots, chunks), out_sha...  54.5 us
    unnamed x1, blocking collectives  7.25 us
    ppermute x1, starting transfers between devices, with_halo(): lax.ppermute(head, axis, [(i + 1, i) for i in range(count - 1)])  4.49 us
    unnamed x16, local copies, waits for them, and re-layouts  4.08 us
    pallas_call x1, Pallas kernels, local(): pl.pallas_call(goldstein_kernel, out_shape=jax.ShapeDtypeStruct((2,) + pl...  3.12 us
    ppermute x1, starting transfers between devices, with_halo(): lax.ppermute(tail, axis, [(i, i + 1) for i in range(count - 1)])  3.02 us
  transfers between devices with their start and end apart: 2, of which 1 were waited for; matrix products, arithmetic and copies ran while one was open for 1% of the time, Pallas kernels for 0%

commit v1 on v0

--- a/solution.py
+++ b/solution.py
@@ -32,15 +32,21 @@
     )
 
 
-def cross_kernel(n, slots, chunks, tab, x, table, out, *scratch):
-    strips = scratch[:chunks]
-    power, ready, landed, own_sem, send_sem, recv_sem, back_send, back_recv = scratch[chunks:]
+def whole_kernel(n, slots, chunks, pairs, position, ranges, x, table_hbm, *rest):
+    tables_hbm, (filtered, magnitude), scratch = rest[:5], rest[5:7], rest[7:]
+    strips, scratch = scratch[:chunks], scratch[chunks:]
+    table, tables, scratch = scratch[0], scratch[1:6], scratch[6:]
+    mine, gathered, tab, power, ready, landed, cells, halo, scratch = *scratch[:8], scratch[8:]
+    own_sem, send_sem, recv_sem, back_send, back_recv, tab_send, tab_recv, table_sem, halo_send, halo_recv = scratch
     me = lax.axis_index("acq")
+    az = lax.axis_index("az")
+    az_count = lax.axis_size("az")
     lines = x.shape[2]
     width = x.shape[3] // n
     looks = width // LR
     step = lines // chunks
     rows = step // LA
+    own = lines // LA
     barrier = pltpu.get_barrier_semaphore()
 
     def peer(k):
@@ -67,6 +73,16 @@
             own_sem.at[c],
         )
 
+    def tab_copy(k):
+        return pltpu.make_async_remote_copy(
+            src_ref=mine,
+            dst_ref=gathered.at[me],
+            send_sem=tab_send.at[k],
+            recv_sem=tab_recv.at[k],
+            device_id={"acq": peer(k)},
+            device_id_type=MESH,
+        )
+
     def back_copy(k):
         return pltpu.make_async_remote_copy(
             src_ref=ready.at[k],
@@ -77,18 +93,61 @@
             device_id_type=MESH,
         )
 
+    def halo_copy(side):
+        return pltpu.make_async_remote_copy(
+            src_ref=cells.at[:, :, pl.ds(0 if side == 0 else own - HALF, HALF)],
+            dst_ref=halo.at[side],
+            send_sem=halo_send.at[side],
+            recv_sem=halo_recv.at[side],
+            device_id={"az": az + (2 * side - 1)},
+            device_id_type=MESH,
+        )
+
+    has = (az > 0, az < az_count - 1)
+    mine[...] = jnp.zeros_like(mine)
+    mine[0:2, 0:slots] = pairs[...]
+    mine[2:4, 0:slots] = ranges[...]
+    mine[4:5, 0:1] = position[...]
     for c in range(chunks):
         own_copy(c).start()
     lax.fori_loop(1, n, greet, 0)
-    pl.semaphore_wait(barrier, n - 1)
+    for side in range(2):
+        @pl.when(has[side])
+        def _(side=side):
+            pl.semaphore_signal(
+                barrier, inc=1, device_id={"az": az + (2 * side - 1)}, device_id_type=MESH
+            )
+    pl.semaphore_wait(barrier, n - 1 + jnp.minimum(az, 1) + jnp.minimum(az_count - 1 - az, 1))
+
+    def send_tab(k, carry):
+        tab_copy(k).start()
+        return carry
+    lax.fori_loop(1, n, send_tab, 0)
     for c in range(chunks):
         def send(k, carry, c=c):
             strip_copy(c, k).start()
             return carry
         lax.fori_loop(1, n, send, 0)
+    loads = [
+        pltpu.make_async_copy(source, target, table_sem.at[i])
+        for i, (source, target) in enumerate(zip((table_hbm, *tables_hbm), (table, *tables)))
+    ]
+    for load in loads:
+        load.start()
 
     lane_slot = lax.broadcasted_iota(jnp.int32, (step, 128), 1) // looks
-    first_line = lax.axis_index("az") * lines
+    first_line = az * lines
+    gathered[me] = mine[...]
+
+    def tab_arrive(k, carry):
+        tab_copy(k).wait_recv()
+        return carry
+    lax.fori_loop(1, n, tab_arrive, 0)
+    to_scalars = pltpu.make_async_copy(gathered, tab, table_sem.at[6])
+    to_scalars.start()
+    to_scalars.wait()
+    for load in loads:
+        load.wait()
     every_slot = table[0]
     for j in range(1, slots):
         every_slot = every_slot + table[j]
@@ -122,15 +181,16 @@
             sec_power = jnp.zeros((step, 128), jnp.float32)
             alive = jnp.zeros((step, 128), jnp.float32)
             for j in range(slots):
-                q = row * slots + j
-                other = slot_of(tab[0, q])
+                other = slot_of(tab[tab[row, 1, j], 4, 0])
                 sec_re = strips[c][other, 0].astype(jnp.float32)
                 sec_im = strips[c][other, 1].astype(jnp.float32)
                 sum_re = sum_re + split_dot(ref_re * sec_re + ref_im * sec_im, table[j])
                 sum_im = sum_im + split_dot(ref_im * sec_re - ref_re * sec_im, table[j])
-                mine = lane_slot == j
-                sec_power = jnp.where(mine, power[other], sec_power)
-                alive = jnp.where(mine & (line >= tab[1, q]) & (line < tab[2, q]), 1.0, alive)
+                own_lanes = lane_slot == j
+                sec_power = jnp.where(own_lanes, power[other], sec_power)
+                alive = jnp.where(
+                    own_lanes & (line >= tab[row, 2, j]) & (line < tab[row, 3, j]), 1.0, alive
+                )
 
             def multilook(values):
                 return jnp.sum((values * alive).reshape(rows, LA, 128), axis=1) / (LA * LR)
@@ -163,8 +223,8 @@
         return carry
     lax.fori_loop(1, n, finish, 0)
 
-    lane = lax.broadcasted_iota(jnp.int32, (3, lines // LA, 128), 2) // looks
-    total = [jnp.zeros((3, lines // LA, 128), jnp.float32) for _ in range(slots)]
+    lane = lax.broadcasted_iota(jnp.int32, (3, own, 128), 2) // looks
+    total = [jnp.zeros((3, own, 128), jnp.float32) for _ in range(slots)]
     for d in range(n):
         piece = jnp.where(me == d, ready[0], landed[d])
         for j in range(slots):
@@ -172,45 +232,82 @@
             moved = pltpu.roll(piece, shift, 2) if shift else piece
             total[j] = jnp.where(lane == d, moved, total[j])
     for j in range(slots):
-        out[:, j] = total[j]
+        cells[:, j] = total[j][:2]
+    for side in range(2):
+        @pl.when(has[side])
+        def _(side=side):
+            halo_copy(side).start()
+    for j in range(slots):
+        magnitude[j] = total[j][2]
 
     def drain(k, carry):
         for c in range(chunks):
             strip_copy(c, k).wait_send()
         back_copy(k).wait_send()
+        tab_copy(k).wait_send()
         return carry
     lax.fori_loop(1, n, drain, 0)
-
-
-def coherences(slc, tab, n, slots):
+    for side in range(2):
+        @pl.when(has[1 - side])
+        def _(side=side):
+            halo_copy(side).wait_recv()
+
+        @pl.when(jnp.logical_not(has[1 - side]))
+        def _(side=side):
+            halo[side] = jnp.zeros(halo.shape[1:], jnp.float32)
+    goldstein(jnp.concatenate([halo[1], cells[...], halo[0]], axis=2), *tables, filtered)
+    for side in range(2):
+        @pl.when(has[side])
+        def _(side=side):
+            halo_copy(side).wait_send()
+
+
+def whole_program(slc, pairs, position, ranges):
+    n = lax.axis_size("acq")
+    slots = pairs.shape[0]
     lines, samples = slc.shape[2:]
     width = samples // n
-    chunks = 2
-    rows = lines // LA
+    chunks = 4
+    own = lines // LA
+    table = look_table(width, slots)
+    tables = goldstein_tables(128)
+    vmem = pl.BlockSpec(memory_space=pltpu.VMEM)
+    hbm = pl.BlockSpec(memory_space=pltpu.HBM)
+    dma = pltpu.SemaphoreType.DMA
     return pl.pallas_call(
-        functools.partial(cross_kernel, n, slots, chunks),
-        out_shape=jax.ShapeDtypeStruct((3, slots, rows, 128), jnp.float32),
-        in_specs=[
-            pl.BlockSpec(memory_space=pltpu.SMEM),
-            pl.BlockSpec(memory_space=pl.ANY),
-            pl.BlockSpec(memory_space=pltpu.VMEM),
-        ],
-        out_specs=pl.BlockSpec(memory_space=pltpu.VMEM),
+        functools.partial(whole_kernel, n, slots, chunks),
+        out_shape=(
+            jax.ShapeDtypeStruct((2, slots, own, 128), jnp.float32),
+            jax.ShapeDtypeStruct((slots, own, 128), jnp.float32),
+        ),
+        in_specs=[vmem] * 3 + [hbm] * (2 + len(tables)),
+        out_specs=(vmem, vmem),
         scratch_shapes=[pltpu.VMEM((n, 2, lines // chunks, width), jnp.bfloat16)] * chunks
+        + [pltpu.VMEM(t.shape, t.dtype) for t in (table, *tables)]
         + [
+            pltpu.VMEM((8, 128), jnp.int32),
+            pltpu.VMEM((n, 8, 128), jnp.int32),
+            pltpu.SMEM((n, 8, 128), jnp.int32),
             pltpu.VMEM((n, lines // chunks, 128), jnp.float32),
-            pltpu.VMEM((n, 3, rows, 128), jnp.float32),
-            pltpu.VMEM((n, 3, rows, 128), jnp.float32),
-            pltpu.SemaphoreType.DMA((chunks,)),
-            pltpu.SemaphoreType.DMA((chunks, n)),
-            pltpu.SemaphoreType.DMA((chunks, n)),
-            pltpu.SemaphoreType.DMA((n,)),
-            pltpu.SemaphoreType.DMA((n,)),
+            pltpu.VMEM((n, 3, own, 128), jnp.float32),
+            pltpu.VMEM((n, 3, own, 128), jnp.float32),
+            pltpu.VMEM((2, slots, own, 128), jnp.float32),
+            pltpu.VMEM((2, 2, slots, HALF, 128), jnp.float32),
+            dma((chunks,)),
+            dma((chunks, n)),
+            dma((chunks, n)),
+            dma((n,)),
+            dma((n,)),
+            dma((n,)),
+            dma((n,)),
+            dma((7,)),
+            dma((2,)),
+            dma((2,)),
         ],
         compiler_params=pltpu.CompilerParams(
-            collective_id=0, has_side_effects=True, vmem_limit_bytes=32 * 2**20
+            collective_id=0, has_side_effects=True, vmem_limit_bytes=63 * 2**20
         ),
-    )(tab, slc, look_table(width, slots))
+    )(pairs.T, position[:, None], ranges.T, slc, table, *tables)
 
 
 def goldstein_tables(columns):
@@ -236,7 +333,7 @@
     return tuple(jnp.asarray(a, jnp.float32) for a in arrays)
 
 
-def goldstein_kernel(cells, left, left_back, forward, backward, ones, out):
+def goldstein(cells, left, left_back, forward, backward, ones, out):
     dot = functools.partial(
         jnp.dot, precision=lax.Precision.HIGHEST, preferred_element_type=jnp.float32
     )
@@ -301,46 +398,9 @@
         out[plane] = result[:, plane * columns : (plane + 1) * columns].reshape(slots, own, columns)
 
 
-def with_halo(cells, axis, dim, width):
-    count = lax.axis_size(axis)
-    head = lax.slice_in_dim(cells, 0, width, axis=dim)
-    tail = lax.slice_in_dim(cells, cells.shape[dim] - width, cells.shape[dim], axis=dim)
-    return jnp.concatenate(
-        [
-            lax.ppermute(tail, axis, [(i, i + 1) for i in range(count - 1)]),
-            cells,
-            lax.ppermute(head, axis, [(i + 1, i) for i in range(count - 1)]),
-        ],
-        axis=dim,
-    )
-
-
-def local(slc, pairs, position, ranges):
-    n = lax.axis_size("acq")
-    slots = pairs.shape[0]
-    mine = jnp.concatenate([pairs[:, 1], ranges[:, 0], ranges[:, 1], position])
-    every = lax.all_gather(mine, "acq", axis=0, tiled=False)
-    sec_time = every[:, :slots].reshape(-1)
-    time_index = jnp.arange(n, dtype=jnp.int32)
-    sec_row = jnp.sum(
-        jnp.where(sec_time[:, None] == time_index[None, :], every[:, 3 * slots][None, :], 0), axis=1
-    )
-    tab = jnp.stack(
-        [sec_row, every[:, slots : 2 * slots].reshape(-1), every[:, 2 * slots : 3 * slots].reshape(-1)]
-    )
-    planes = coherences(slc, tab, n, slots)
-    extended = with_halo(planes[:2], "az", 2, HALF)
-    filtered = pl.pallas_call(
-        goldstein_kernel,
-        out_shape=jax.ShapeDtypeStruct((2,) + planes.shape[1:], jnp.float32),
-        compiler_params=pltpu.CompilerParams(vmem_limit_bytes=32 * 2**20),
-    )(extended, *goldstein_tables(planes.shape[-1]))
-    return (filtered, planes[2])
-
-
 def solution(mesh):
     return jax.shard_map(
-        local,
+        whole_program,
         mesh=mesh,
         in_specs=(
             P(None, ("groups", "acq"), "az", None),

time: 81.7 us -> 69.3 us (0.85)
  starting transfers between devices: 7.51 us -> 0 us
  Pallas kernels: 57.6 us -> 64.9 us
  blocking collectives: 7.25 us -> 0 us
  local copies, waits for them, and re-layouts: 6.05 us -> 2.85 us
    ppermute x2 -> x0, starting transfers between devices: 7.51 us -> none  [the longest x1 4.49 us: with_halo(): lax.ppermute(head, axis, [(i + 1, i) for i in range(count - 1)])]
    pallas_call x2 -> x1, Pallas kernels: 57.6 us -> 64.9 us  [whole_program(): pl.pallas_call(functools.partial(whole_kernel, n, slots, chunks), out_sha...]
    unnamed x1 -> x0, blocking collectives: 7.25 us -> none
    squeeze x2 -> x0, local copies, waits for them, and re-layouts: 1.38 us -> none  [the longest x1 0.76 us: local(): mine = jnp.concatenate([pairs[:, 1], ranges[:, 0], ranges[:, 1], position])]
    unnamed x16 -> x2, local copies, waits for them, and re-layouts: 4.08 us -> 2.85 us
  transfers between devices with their start and end apart: 2 -> 0, of which waited for: 1 -> 0; matrix products, arithmetic and copies ran while one was open for 1% -> 0% of each run, Pallas kernels for 0% -> 0%
where the time goes in v1:
time: 69.3 us; the launch traced here: 69 us
  Pallas kernels  64.9 us (94%)
  local copies, waits for them, and re-layouts  2.85 us (4%)
  between operations  1.28 us (2%)
    pallas_call x1, Pallas kernels, whole_program(): pl.pallas_call(functools.partial(whole_kernel, n, slots, chunks), out_sha...  64.9 us
    unnamed x2, local copies, waits for them, and re-layouts  2.85 us

profile of v1, /device:TPU:1, one launch (start us, length us, event | category | flops | bytes accessed | tf_op | source)
XLA Modules:
  0.0 69.0 jit_solution(14990449881025855126)
XLA Ops:
  1.3 64.9 %shard_map.113 = (f32[2,4,16,128]{3,2,1,0:T(8,128)}, f32[4,16,128]{2,1,0:T(8,128)}) custom-call(s32[2,4]{1,0:T(2,128)} %bitcast.4, s32[1,1]{1,0:T(1,128)} %bitcast.3.position, s32[2,4]{1,0:T(2,128)} %bitcast.5, bf16[2,1,128,4096]{3,2,1,0:T(8,128)(2,1)} %x.1, bf16[4,1024,128]{2,1,0:T(8,128)(2,1)} %constant.12.clone.table_hbm, ...), custom_call_target="tpu_custom_call" | custom-call | tf_op jit(solution)/shard_map/pallas_call | solution.py:277
  66.2 1.5 %copy.15 = f32[2,4,16,128]{3,2,1,0:T(8,128)} copy(f32[2,4,16,128]{3,2,1,0:T(8,128)} %get-tuple-element.4) | data formatting | bytes 131072
  67.7 1.4 %copy.16 = f32[4,16,128]{2,1,0:T(8,128)} copy(f32[4,16,128]{2,1,0:T(8,128)} %get-tuple-element.5) | data formatting | bytes 65536

commit v2 on v1

--- a/solution.py
+++ b/solution.py
@@ -18,18 +18,19 @@
 
 def look_table(width, slots):
     looks = width // LR
-    table = np.zeros((slots, width, 128), np.float32)
+    table = np.zeros((width, 128), np.float32)
     for j in range(slots):
-        table[j, np.arange(width), j * looks + np.arange(width) // LR] = 1.0
+        table[np.arange(width), j * looks + np.arange(width) // LR] = 1.0
     return jnp.asarray(table, jnp.bfloat16)
 
 
 def split_dot(values, table):
     high = values.astype(jnp.bfloat16)
     low = (values - high.astype(jnp.float32)).astype(jnp.bfloat16)
-    return jnp.dot(high, table, preferred_element_type=jnp.float32) + jnp.dot(
-        low, table, preferred_element_type=jnp.float32
-    )
+    both = jnp.dot(
+        jnp.concatenate([high, low], axis=0), table, preferred_element_type=jnp.float32
+    )
+    return both[: values.shape[0]] + both[values.shape[0] :]
 
 
 def whole_kernel(n, slots, chunks, pairs, position, ranges, x, table_hbm, *rest):
@@ -124,10 +125,10 @@
         return carry
     lax.fori_loop(1, n, send_tab, 0)
     for c in range(chunks):
-        def send(k, carry, c=c):
-            strip_copy(c, k).start()
+        def send(i, carry, c=c):
+            strip_copy(c, 1 + lax.rem(i + n // 2 - 1, n - 1)).start()
             return carry
-        lax.fori_loop(1, n, send, 0)
+        lax.fori_loop(0, n - 1, send, 0)
     loads = [
         pltpu.make_async_copy(source, target, table_sem.at[i])
         for i, (source, target) in enumerate(zip((table_hbm, *tables_hbm), (table, *tables)))
@@ -148,10 +149,6 @@
     to_scalars.wait()
     for load in loads:
         load.wait()
-    every_slot = table[0]
-    for j in range(1, slots):
-        every_slot = every_slot + table[j]
-
     def slot_of(row):
         return lax.rem(me - row + n, n)
 
@@ -167,7 +164,7 @@
         def powers(k, carry, c=c):
             re = strips[c][k, 0].astype(jnp.float32)
             im = strips[c][k, 1].astype(jnp.float32)
-            power[k] = split_dot(re * re + im * im, every_slot)
+            power[k] = split_dot(re * re + im * im, table[...])
             return carry
         lax.fori_loop(0, n, powers, 0)
 
@@ -180,17 +177,24 @@
             sum_im = jnp.zeros((step, 128), jnp.float32)
             sec_power = jnp.zeros((step, 128), jnp.float32)
             alive = jnp.zeros((step, 128), jnp.float32)
+            products = []
             for j in range(slots):
                 other = slot_of(tab[tab[row, 1, j], 4, 0])
                 sec_re = strips[c][other, 0].astype(jnp.float32)
                 sec_im = strips[c][other, 1].astype(jnp.float32)
-                sum_re = sum_re + split_dot(ref_re * sec_re + ref_im * sec_im, table[j])
-                sum_im = sum_im + split_dot(ref_im * sec_re - ref_re * sec_im, table[j])
+                products.append(ref_re * sec_re + ref_im * sec_im)
+                products.append(ref_im * sec_re - ref_re * sec_im)
                 own_lanes = lane_slot == j
                 sec_power = jnp.where(own_lanes, power[other], sec_power)
                 alive = jnp.where(
                     own_lanes & (line >= tab[row, 2, j]) & (line < tab[row, 3, j]), 1.0, alive
                 )
+            sums = split_dot(jnp.concatenate(products, axis=0), table[...])
+            for j in range(slots):
+                own_lanes = lane_slot == j
+                at_re = 2 * j * step
+                sum_re = jnp.where(own_lanes, sums[at_re : at_re + step], sum_re)
+                sum_im = jnp.where(own_lanes, sums[at_re + step : at_re + 2 * step], sum_im)
 
             def multilook(values):
                 return jnp.sum((values * alive).reshape(rows, LA, 128), axis=1) / (LA * LR)

time: 69.3 us -> 68.4 us (0.987)
  Pallas kernels: 64.9 us -> 64 us
    pallas_call x1, Pallas kernels: 64.9 us -> 64 us  [whole_program(): pl.pallas_call(functools.partial(whole_kernel, n, slots, chunks), out_sha...]
where the time goes in v2:
time: 68.4 us; the launch traced here: 68.1 us
  Pallas kernels  64 us (94%)
  local copies, waits for them, and re-layouts  2.85 us (4%)
  between operations  1.28 us (2%)
    pallas_call x1, Pallas kernels, whole_program(): pl.pallas_call(functools.partial(whole_kernel, n, slots, chunks), out_sha...  64 us
    unnamed x2, local copies, waits for them, and re-layouts  2.85 us

profile of v2, /device:TPU:1, one launch (start us, length us, event | category | flops | bytes accessed | tf_op | source)
XLA Modules:
  0.0 68.1 jit_solution(12770896112564552467)
XLA Ops:
  1.3 64.0 %shard_map.113 = (f32[2,4,16,128]{3,2,1,0:T(8,128)}, f32[4,16,128]{2,1,0:T(8,128)}) custom-call(s32[2,4]{1,0:T(2,128)} %bitcast.4, s32[1,1]{1,0:T(1,128)} %bitcast.3.position, s32[2,4]{1,0:T(2,128)} %bitcast.5, bf16[2,1,128,4096]{3,2,1,0:T(8,128)(2,1)} %x.1, bf16[1024,128]{1,0:T(8,128)(2,1)} %constant.12.clone.table_hbm, f32[64,64]{1,0:T(8,128)} %constant.13.clone.rest_0_, ...), custom_call_target="tpu_custom_call" | custom-call | tf_op jit(solution)/shard_map/pallas_call | solution.py:281
  65.3 1.5 %copy.15 = f32[2,4,16,128]{3,2,1,0:T(8,128)} copy(f32[2,4,16,128]{3,2,1,0:T(8,128)} %get-tuple-element.4) | data formatting | bytes 131072
  66.8 1.4 %copy.16 = f32[4,16,128]{2,1,0:T(8,128)} copy(f32[4,16,128]{2,1,0:T(8,128)} %get-tuple-element.5) | data formatting | bytes 65536

commit v3 on v2

--- a/solution.py
+++ b/solution.py
@@ -34,7 +34,7 @@
 
 
 def whole_kernel(n, slots, chunks, pairs, position, ranges, x, table_hbm, *rest):
-    tables_hbm, (filtered, magnitude), scratch = rest[:5], rest[5:7], rest[7:]
+    tables_hbm, out, scratch = rest[:5], rest[5], rest[6:]
     strips, scratch = scratch[:chunks], scratch[chunks:]
     table, tables, scratch = scratch[0], scratch[1:6], scratch[6:]
     mine, gathered, tab, power, ready, landed, cells, halo, scratch = *scratch[:8], scratch[8:]
@@ -105,12 +105,6 @@
         )
 
     has = (az > 0, az < az_count - 1)
-    mine[...] = jnp.zeros_like(mine)
-    mine[0:2, 0:slots] = pairs[...]
-    mine[2:4, 0:slots] = ranges[...]
-    mine[4:5, 0:1] = position[...]
-    for c in range(chunks):
-        own_copy(c).start()
     lax.fori_loop(1, n, greet, 0)
     for side in range(2):
         @pl.when(has[side])
@@ -118,6 +112,12 @@
             pl.semaphore_signal(
                 barrier, inc=1, device_id={"az": az + (2 * side - 1)}, device_id_type=MESH
             )
+    mine[...] = jnp.zeros_like(mine)
+    mine[0:2, 0:slots] = pairs[...]
+    mine[2:4, 0:slots] = ranges[...]
+    mine[4:5, 0:1] = position[...]
+    for c in range(chunks):
+        own_copy(c).start()
     pl.semaphore_wait(barrier, n - 1 + jnp.minimum(az, 1) + jnp.minimum(az_count - 1 - az, 1))
 
     def send_tab(k, carry):
@@ -242,7 +242,7 @@
         def _(side=side):
             halo_copy(side).start()
     for j in range(slots):
-        magnitude[j] = total[j][2]
+        out[2, j] = total[j][2]
 
     def drain(k, carry):
         for c in range(chunks):
@@ -259,7 +259,7 @@
         @pl.when(jnp.logical_not(has[1 - side]))
         def _(side=side):
             halo[side] = jnp.zeros(halo.shape[1:], jnp.float32)
-    goldstein(jnp.concatenate([halo[1], cells[...], halo[0]], axis=2), *tables, filtered)
+    goldstein(jnp.concatenate([halo[1], cells[...], halo[0]], axis=2), *tables, out)
     for side in range(2):
         @pl.when(has[side])
         def _(side=side):
@@ -278,14 +278,11 @@
     vmem = pl.BlockSpec(memory_space=pltpu.VMEM)
     hbm = pl.BlockSpec(memory_space=pltpu.HBM)
     dma = pltpu.SemaphoreType.DMA
-    return pl.pallas_call(
+    planes = pl.pallas_call(
         functools.partial(whole_kernel, n, slots, chunks),
-        out_shape=(
-            jax.ShapeDtypeStruct((2, slots, own, 128), jnp.float32),
-            jax.ShapeDtypeStruct((slots, own, 128), jnp.float32),
-        ),
+        out_shape=jax.ShapeDtypeStruct((3, slots, own, 128), jnp.float32),
         in_specs=[vmem] * 3 + [hbm] * (2 + len(tables)),
-        out_specs=(vmem, vmem),
+        out_specs=vmem,
         scratch_shapes=[pltpu.VMEM((n, 2, lines // chunks, width), jnp.bfloat16)] * chunks
         + [pltpu.VMEM(t.shape, t.dtype) for t in (table, *tables)]
         + [
@@ -312,6 +309,7 @@
             collective_id=0, has_side_effects=True, vmem_limit_bytes=63 * 2**20
         ),
     )(pairs.T, position[:, None], ranges.T, slc, table, *tables)
+    return (planes[:2], planes[2])
 
 
 def goldstein_tables(columns):

time: 68.4 us -> 68.4 us (level)
    unnamed x2 -> x0, local copies, waits for them, and re-layouts: 2.85 us -> none
    slice x0 -> x1, local copies, waits for them, and re-layouts: none -> 1.47 us  [whole_program(): return (planes[:2], planes[2])]
    squeeze x0 -> x1, local copies, waits for them, and re-layouts: none -> 1.38 us  [whole_program(): return (planes[:2], planes[2])]
where the time goes in v3:
time: 68.4 us; the launch traced here: 68.1 us
  Pallas kernels  64 us (94%)
  local copies, waits for them, and re-layouts  2.85 us (4%)
  between operations  1.28 us (2%)
    pallas_call x1, Pallas kernels, whole_program(): pl.pallas_call(functools.partial(whole_kernel, n, slots, chunks), out_sha...  64 us
    slice x1, local copies, waits for them, and re-layouts, whole_program(): return (planes[:2], planes[2])  1.47 us
    squeeze x1, local copies, waits for them, and re-layouts, whole_program(): return (planes[:2], planes[2])  1.38 us

profile of v3, /device:TPU:1, one launch (start us, length us, event | category | flops | bytes accessed | tf_op | source)
XLA Modules:
  0.0 68.1 jit_solution(14277725763190731752)
XLA Ops:
  1.3 64.0 %shard_map.113 = f32[3,4,16,128]{3,2,1,0:T(8,128)} custom-call(s32[2,4]{1,0:T(2,128)} %bitcast.6, s32[1,1]{1,0:T(1,128)} %bitcast.5.position, s32[2,4]{1,0:T(2,128)} %bitcast.7, bf16[2,1,128,4096]{3,2,1,0:T(8,128)(2,1)} %x.1, bf16[1024,128]{1,0:T(8,128)(2,1)} %constant.12.clone.table_hbm, f32[64,64]{1,0:T(8,128)} %constant.13.clone.rest_0_, ...), custom_call_target="tpu_custom_call" | custom-call | tf_op jit(solution)/shard_map/pallas_call | solution.py:281
  65.3 1.4 %slice_bitcast_fusion = f32[4,16,128]{2,1,0:T(8,128)} fusion(f32[3,4,16,128]{3,2,1,0:T(8,128)} %shard_map.113), kind=kLoop, calls=%fused_computation | loop fusion | bytes 65536 | tf_op jit(solution)/shard_map/squeeze | solution.py:312
  66.7 1.5 %slice.6 = f32[2,4,16,128]{3,2,1,0:T(8,128)} slice(f32[3,4,16,128]{3,2,1,0:T(8,128)} %shard_map.113), slice={[0:2], [0:4], [0:16], [0:128]} | slice | bytes 131072 | tf_op jit(solution)/shard_map/slice | solution.py:312
